TPU v7x, 32 devices: a whole 2x2x4 slice. The times are simulated.
32 devices in a mesh: dp: 8 (over z, x), rep: 4 (over y, core).
Axes of the slice: x: 2, y: 2, z: 4, core: 2. Of those that a mesh axis runs over, the one named last changes fastest.
Arguments:
- frames_in: bfloat16 [4, 7168, 1536], P('rep', 'dp')
- lengths: int32 [4, 8, 4], P('rep', 'dp'), may hold values from 1 to 893, as said below
- norm_gain: float32 [1536], replicated, may hold values from 0.5 to 1.5
- norm_bias: float32 [1536], replicated, may hold values from -2 to 2
- w_in: bfloat16 [1536, 3072], P(('dp', 'rep')), may hold values from -0.15625 to 0.15625
- kernel: float32 [31, 1536], replicated, may hold values from -1 to 1
- batch_gain: float32 [1536], replicated, may hold values from 0.5 to 1.5
- batch_bias: float32 [1536], replicated, may hold values from -3 to 3
- w_out: bfloat16 [1536, 1536], P(('dp', 'rep')), may hold values from -0.15625 to 0.15625
Outputs:
- frames_out: bfloat16 [4, 7168, 1536], P('rep', 'dp')
Inputs may be any that keep to these rules, and one draw needn't show every extreme that they name: `lengths`: for each rep index, the devices 2k and 2k + 1 of dp hold 1024 frames together, so each rep index holds 512 frames for each of its dp devices; a device holds at most 896 frames, and some device of every rep index holds exactly 896.
All inputs are finite; a program needn't handle non-finite values.
Results may differ from a plain program's by a relative error of at most 0.0038.
Values may be sent and summed in bfloat16 or wider, within the bound.
No kernel may reach another device: no remote copies, remote signals or barrier semaphores. Data moves between devices by JAX's collectives and lax.ppermute only.
A program may use at most 128 MiB of HBM per device.

v0:
```python
import jax
import jax.numpy as jnp
from jax import lax
from jax.sharding import PartitionSpec as P

FR_DEV = 512


EPSILON = 1e-05


def layer_norm(frames, norm_gain, norm_bias):
    values = frames.astype(jnp.float32)
    average = jnp.mean(values, axis=-1, keepdims=True)
    centred = values - average
    spread = jnp.mean(centred * centred, axis=-1, keepdims=True)
    return centred * lax.rsqrt(spread + EPSILON) * norm_gain + norm_bias


def depthwise(gated, labels, kernel):
    half_kernel = kernel.shape[0] // 2
    length_rows = gated.shape[0]
    padded = jnp.pad(gated, ((half_kernel, half_kernel), (0, 0)))
    padded_labels = jnp.pad(labels, (half_kernel, half_kernel), constant_values=-1)
    summed = jnp.zeros(gated.shape, jnp.float32)
    for offset in range(kernel.shape[0]):
        shared = padded_labels[offset : offset + length_rows] == labels
        contribution = jnp.where(
            shared[:, None], padded[offset : offset + length_rows].astype(jnp.float32), 0.0
        )
        summed = summed + contribution * kernel[offset]
    return summed


def project_in(normed, weight_rows):
    return jnp.dot(normed, weight_rows, preferred_element_type=jnp.float32)


def project_out(active, weight_rows):
    return jnp.dot(active, weight_rows, preferred_element_type=jnp.float32)


def on_device(
    frames_in, lengths, norm_gain, norm_bias, w_in, kernel, batch_gain, batch_bias, w_out
):
    local_frames = frames_in[0]
    local_lengths = lengths[0, 0]
    capacity = local_frames.shape[0]
    features = local_frames.shape[1]
    total_count = lax.axis_size("dp") * lax.axis_size("rep") * FR_DEV
    grouped = (w_in, w_out)
    grouped = (
        lax.all_gather(w_in, ("dp", "rep"), axis=0, tiled=True),
        lax.all_gather(w_out, ("dp", "rep"), axis=0, tiled=True),
    )
    rows_here = jnp.arange(capacity, dtype=jnp.int32)
    local_load = jnp.sum(local_lengths)
    bounds = jnp.cumsum(local_lengths)
    labels = jnp.sum((rows_here[:, None] >= bounds[None, :]).astype(jnp.int32), axis=1)
    row_weight = (rows_here < local_load).astype(jnp.float32)[:, None]
    normed = layer_norm(local_frames, norm_gain, norm_bias).astype(jnp.bfloat16)
    projected = project_in(normed, grouped[0])
    gated = (projected[:, :features] * jax.nn.sigmoid(projected[:, features:])).astype(jnp.bfloat16)
    convolved = depthwise(gated, labels, kernel)
    average = lax.psum(jnp.sum(convolved * row_weight, axis=0), ("dp", "rep")) / total_count
    centred = convolved - average
    spread = lax.psum(jnp.sum(centred * centred * row_weight, axis=0), ("dp", "rep")) / total_count
    scaled = centred * lax.rsqrt(spread + EPSILON) * batch_gain + batch_bias
    active = jax.nn.silu(scaled).astype(jnp.bfloat16)
    branch = project_out(active, grouped[1])
    mixed = (local_frames.astype(jnp.float32) + branch).astype(jnp.bfloat16)
    result = jnp.where(rows_here[:, None] < local_load, mixed, jnp.zeros_like(mixed))
    return result[None]


def solution(mesh):
    placed = (
        P("rep", "dp", None),
        P("rep", "dp", None),
        P(),
        P(),
        P(("dp", "rep"), None),
        P(),
        P(),
        P(),
        P(("dp", "rep"), None),
    )
    return jax.shard_map(
        on_device, mesh=mesh, in_specs=placed, out_specs=P("rep", "dp", None), check_vma=False
    )
```

profile of v0, /device:TPU:0, one launch (start us, length us, event | category | flops | bytes accessed | tf_op | source)
XLA Modules:
  0.0 246.4 jit_solution(14856618162979881424)
XLA Ops:
  6.5 0.7 all-gather.3.cloned.1.call-update
  7.3 0.0 all-gather.5.cloned.1.call-start
  7.3 0.7 all-gather.5.cloned.1.call-update
  8.0 1.8 slice_reduce_fusion.30
  9.8 1.4 slice_reduce_fusion.29
  11.2 0.8 reduce-window.8
  12.0 0.1 convert_reduce_fusion.1
  12.1 0.1 slice_compare_fusion.29
  12.2 0.1 slice_compare_fusion.28
  12.3 0.1 slice_compare_fusion.27
  12.4 1.3 reduce_sum.54
  13.7 0.7 slice_compare_fusion.26
  14.4 0.7 iota_compare_fusion.1
  15.1 2.2 convert_reduce_fusion
  17.3 0.9 fusion.4
  18.2 77.0 %all-gather.3.cloned.1.call-done = bf16[1536,3072]{1,0:T(8,128)(2,1)} async-done(((bf16[48,3072]{1,0:T(8,128)(2,1)}), bf16[1536,3072]{1,0:T(8,128)(2,1)}) %all-gather.3.cloned.1.call-update) | async-done | bytes 9437200 | tf_op jit(solution)/shard_map/all_gather | solution.py:53
  95.1 11.4 %fusion.16 = f32[896,3072]{1,0:T(8,128)S(1)} fusion(bf16[1536,3072]{1,0:T(8,128)(2,1)} %all-gather.3.cloned.1.call-done, bf16[1,896,1536]{2,1,0:T(8,128)(2,1)S(1)} %copy-done, f32[1536]{0:T(1024)S(1)} %copy-done.2, f32[1536]{0:T(1024)S(1)} %copy-done.3, f32[896]{0:T(1024)S(1)} %add_rsqrt_fusion.1, f32[896]{0:T(1024)S(1)} %broadcast_multiply_fusion.1), kind=kOutput, calls=%fused_computation.23 | convolution fusion | flops 8463974400 | bytes 23219200 | tf_op jit(solution)/shard_map/dot_general | solution.py:36
  106.6 1.5 fusion.13
  108.1 38.2 %multiply_reduce_fusion.1 = (f32[1536]{0:T(1024)S(1)}, f32[896,1536]{1,0:T(8,128)}) fusion(f32[896]{0:T(1024)S(1)} %get-tuple-element.68, f32[1536]{0:T(1024)S(1)} %get-tuple-element.34, pred[896]{0:T(1024)(128)(4,1)S(1)} %get-tuple-element.67, f32[1536]{0:T(1024)S(1)} %get-tuple-element.35, pred[896]{0:T(1024)(128)(4,1)S(1)} %get-tuple-element.39, ...), kind=kLoop, calls=%fused_computation.18 | loop fusion | flops 170654208 | bytes 8484608 | tf_op jit(solution)/shard_map/reduce_sum | solution.py:65
  146.3 39.3 %psum.14 = f32[1536]{0:T(1024)S(1)} all-reduce(f32[1536]{0:T(1024)S(1)} %get-tuple-element.36), channel_id=1, replica_groups=mesh['dp'=8,'rep'=4] {'dp','rep'}, use_global_device_ids=true, to_apply=%region_6.7 | all-reduce | flops 1536 | bytes 12288 | tf_op jit(solution)/shard_map/psum | solution.py:65
  185.5 3.3 %multiply_reduce_fusion = f32[1536]{0:T(1024)S(1)} fusion(f32[896,1536]{1,0:T(8,128)} %get-tuple-element.37, f32[1536]{0:T(1024)S(1)} %broadcast_multiply_fusion, f32[896]{0:T(1024)S(1)} %get-tuple-element.68), kind=kLoop, calls=%fused_computation.17 | loop fusion | flops 5503488 | bytes 5520896 | tf_op jit(solution)/shard_map/reduce_sum | solution.py:67
  188.8 40.2 %psum.15 = f32[1536]{0:T(1024)S(1)} all-reduce(f32[1536]{0:T(1024)S(1)} %multiply_reduce_fusion), channel_id=1, replica_groups=mesh['dp'=8,'rep'=4] {'dp','rep'}, use_global_device_ids=true, to_apply=%region_8.9 | all-reduce | flops 1536 | bytes 12288 | tf_op jit(solution)/shard_map/psum | solution.py:67
  229.1 0.0 all-gather.5.cloned.1.call-done
  229.1 10.5 %fusion.15 = bf16[1,896,1536]{2,1,0:T(8,128)(2,1)} fusion(bf16[1536,1536]{1,0:T(8,128)(2,1)} %all-gather.5.cloned.1.call-done, bf16[1,896,1536]{2,1,0:T(8,128)(2,1)S(1)} %copy-done.1, f32[896,1536]{1,0:T(8,128)} %get-tuple-element.37, f32[1536]{0:T(1024)S(1)} %copy-done.4, f32[1536]{0:T(1024)S(1)} %copy-done.5, f32[1536]{0:T(1024)S(1)} %add_rsqrt_fusion, ...), kind=kOutput, calls=%fused_computation.22 | convolution fusion | flops 4245749760 | bytes 15754112 | tf_op jit(solution)/shard_map/dot_general | solution.py:40
  (17 shorter events, 0.1 us)
Async XLA Ops:
  6.5 10.7 %copy-start = (bf16[1,896,1536]{2,1,0:T(8,128)(2,1)S(1)}, bf16[1,896,1536]{2,1,0:T(8,128)(2,1)}, u32[]{:S(2)}) copy-start(bf16[1,896,1536]{2,1,0:T(8,128)(2,1)} %param.9) | copy-start | bytes 8257540
  6.5 88.6 %copy-start.3 = (f32[1536]{0:T(1024)S(1)}, f32[1536]{0:T(1024)}, u32[]{:S(2)}) copy-start(f32[1536]{0:T(1024)} %param.11) | copy-start | bytes 18436
  6.5 88.6 %copy-start.2 = (f32[1536]{0:T(1024)S(1)}, f32[1536]{0:T(1024)}, u32[]{:S(2)}) copy-start(f32[1536]{0:T(1024)} %param.12) | copy-start | bytes 18436
  6.5 88.6 %all-gather.3.cloned.1.call-start = ((), (), s32[]{:S(2)}) async-start(), calls=%async_computation | async-start | bytes 9732096 | tf_op jit(solution)/shard_map/all_gather | solution.py:53
  7.3 221.8 %all-gather.5.cloned.1.call-start = ((), (), s32[]{:S(2)}) async-start(), calls=%async_computation.1 | async-start | bytes 4866048 | tf_op jit(solution)/shard_map/all_gather | solution.py:54
  108.1 121.0 %copy-start.4 = (f32[1536]{0:T(1024)S(1)}, f32[1536]{0:T(1024)}, u32[]{:S(2)}) copy-start(f32[1536]{0:T(1024)} %param.16) | copy-start | bytes 18436
  108.1 121.0 %copy-start.5 = (f32[1536]{0:T(1024)S(1)}, f32[1536]{0:T(1024)}, u32[]{:S(2)}) copy-start(f32[1536]{0:T(1024)} %param.15) | copy-start | bytes 18436
  146.3 82.8 %copy-start.1 = (bf16[1,896,1536]{2,1,0:T(8,128)(2,1)S(1)}, bf16[1,896,1536]{2,1,0:T(8,128)(2,1)}, u32[]{:S(2)}) copy-start(bf16[1,896,1536]{2,1,0:T(8,128)(2,1)} %param.9) | copy-start | bytes 8257540
Sparse Core Ops, SparseCore 0:
  10.3 84.7 all-gather.2
  98.0 62.1 all-gather.4
where the time goes:
time: 247 us; the launch traced here: 246 us
  blocking collectives  79.5 us (32%)
  waiting for transfers between devices  78.4 us (32%)
  other arithmetic  49.9 us (20%)
  matrix products  21.9 us (9%)
  between operations  13.5 us (5%)
  local copies, waits for them, and re-layouts  3.21 us (1%)
    all_gather x1, waiting for transfers between devices, on_device(): lax.all_gather(w_in, ('dp', 'rep'), axis=0, tiled=True)  77 us
    psum x1, blocking collectives, on_device(): lax.psum(jnp.sum(centred * centred * row_weight, axis=0), ('dp', 'rep'))  40.2 us
    psum x1, blocking collectives, on_device(): lax.psum(jnp.sum(convolved * row_weight, axis=0), ('dp', 'rep'))  39.3 us
    reduce_sum x1, other arithmetic, on_device(): jnp.sum(convolved * row_weight, axis=0)  38.2 us
    dot_general x1, matrix products, project_in(): return jnp.dot(normed, weight_rows, preferred_element_type=jnp.float32)  11.4 us
    dot_general x1, matrix products, project_out(): return jnp.dot(active, weight_rows, preferred_element_type=jnp.float32)  10.5 us
  transfers between devices with their start and end apart: 2, of which 1 were waited for; matrix products, arithmetic and copies ran while one was open for 26% of the time, Pallas kernels for 0%

commit v1 on v0

v1 whole, which is shorter than its diff:
```python
import functools

import jax
import jax.numpy as jnp
import numpy as np
from jax import lax
from jax.experimental import pallas as pl
from jax.experimental.pallas import tpu as pltpu
from jax.sharding import PartitionSpec as P

FR_DEV = 512
EPSILON = 1e-05
AXES = ("dp", "rep")
GAP = 16
LANES = 128
VMEM_LIMIT = 48 * 1024 * 1024


def round_up(value, step):
    return -(-value // step) * step


class Grid:
    def __init__(self, n_dp, n_rep):
        self.n_dp, self.n_rep = n_dp, n_rep
        self.x = 2 if n_dp % 2 == 0 else 1
        self.z = n_dp // self.x
        self.c = 2 if n_rep % 2 == 0 else 1
        self.y = n_rep // self.c
        self.count = n_dp * n_rep

    def pairs(self, target):
        found = []
        for d in range(self.n_dp):
            for r in range(self.n_rep):
                z, x = divmod(d, self.x)
                y, c = divmod(r, self.c)
                tz, tx, ty, tc = target(z, x, y, c)
                found.append((d * self.n_rep + r, (tz * self.x + tx) * self.n_rep + ty * self.c + tc))
        return found


class Held:
    def __init__(self, value, owners):
        self.value, self.owners = value, owners

    def sent(self, pairs):
        owners = [None] * len(self.owners)
        for source, target in pairs:
            owners[target] = self.owners[source]
        return Held(lax.ppermute(self.value, AXES, pairs), owners)


def joined(*parts):
    owners = [sum((list(p.owners[i]) for p in parts), []) for i in range(len(parts[0].owners))]
    return Held(jnp.concatenate([p.value for p in parts], axis=0), owners)


def z_ring(grid, held):
    step = grid.pairs(lambda z, x, y, c: ((z + 1) % grid.z, x, y, c))
    parts = [held]
    for _ in range(grid.z - 1):
        parts.append(parts[-1].sent(step))
    return joined(*parts)


def xy_swap(grid, held):
    first = grid.pairs(lambda z, x, y, c: (z, x ^ 1, y, c) if c == 0 else (z, x, y ^ 1, c))
    second = grid.pairs(lambda z, x, y, c: (z, x, y ^ 1, c) if c == 0 else (z, x ^ 1, y, c))
    held = joined(held, held.sent(first))
    return joined(held, held.sent(second))


def gather(grid, shard, z_first):
    held = Held(shard, [[i] for i in range(grid.count)])
    if z_first:
        held = xy_swap(grid, z_ring(grid, held))
    else:
        held = z_ring(grid, xy_swap(grid, held))
    other = held.sent(grid.pairs(lambda z, x, y, c: (z, x, y, c ^ 1)))
    return (held, other)


def place_of(pieces, me):
    table = np.concatenate([np.asarray(p.owners, np.int32) for p in pieces], axis=1)
    return jnp.asarray(table)[me]


def row_bounds(lengths_ref, utterances):
    bounds, total = [0], 0
    for u in range(utterances):
        total = total + lengths_ref[u]
        bounds.append(total)
    return bounds


def norm_kernel(lengths_ref, frames_ref, gain_ref, bias_ref, out_ref, mask_ref, scratch, *, utterances):
    rows = frames_ref.shape[0]
    bounds = row_bounds(lengths_ref, utterances)
    lead = (utterances - 1) * GAP
    width = frames_ref.shape[1]
    scratch[0:lead, :] = jnp.zeros((lead, width), scratch.dtype)
    tail = scratch.shape[0] - lead - rows
    scratch[lead + rows : lead + rows + tail, :] = jnp.zeros((tail, width), scratch.dtype)
    step = 32
    assert rows % step == 0

    @pl.loop(0, rows // step)
    def _(i):
        start = pl.multiple_of(i * step, step)
        values = frames_ref[pl.ds(start, step), :].astype(jnp.float32)
        average = jnp.mean(values, axis=-1, keepdims=True)
        centred = values - average
        spread = jnp.mean(centred * centred, axis=-1, keepdims=True)
        normed = centred * lax.rsqrt(spread + EPSILON) * gain_ref[...] + bias_ref[...]
        scratch[pl.ds(lead + start, step), :] = normed.astype(scratch.dtype)

    @pl.loop(0, out_ref.shape[0] // GAP)
    def _(i):
        start = pl.multiple_of(i * GAP, GAP)
        placed = jnp.zeros((GAP, width), jnp.float32)
        live = jnp.zeros((GAP, LANES), jnp.float32)
        for u in range(utterances):
            row = lax.broadcasted_iota(jnp.int32, (GAP, LANES), 0) + (start - u * GAP)
            inside = (row >= bounds[u]) & (row < bounds[u + 1])
            live = jnp.where(inside, 1.0, live)
            wide = jnp.broadcast_to(inside[:, :1], (GAP, width))
            block = scratch[pl.ds(pl.multiple_of(lead + start - u * GAP, GAP), GAP), :]
            placed = jnp.where(wide, block.astype(jnp.float32), placed)
        out_ref[pl.ds(start, GAP), :] = placed.astype(out_ref.dtype)
        mask_ref[pl.ds(start, GAP), :] = live


def sigmoid(value):
    return 0.5 * jnp.tanh(0.5 * value) + 0.5


def reorder(places_ref, pieces, target):
    shard = sum(p.shape[0] for p in pieces) // places_ref.shape[0]
    at = 0
    for piece in pieces:
        for i in range(piece.shape[0] // shard):
            to = pl.multiple_of(places_ref[at] * shard, 16)
            target[pl.ds(to, shard), :] = piece[i * shard : (i + 1) * shard, :]
            at += 1


def chunk_kernel(*refs, n_pieces, row_tile, halo):
    places_ref, count_ref, normed_ref, mask_ref, taps_ref = refs[:5]
    pieces = refs[5 : 5 + n_pieces]
    conv_ref, stats_ref, weights, gated = refs[5 + n_pieces :]
    rows, depth = normed_ref.shape
    channels = weights.shape[1] // 2
    groups = channels // LANES
    n_taps = taps_ref.shape[0]
    half = n_taps // 2
    reorder(places_ref, pieces, weights)
    for g in range(groups):
        gated[g, 0:halo, :] = jnp.zeros((halo, LANES), jnp.float32)
        gated[g, halo + rows : halo + rows + halo, :] = jnp.zeros((halo, LANES), jnp.float32)

    @pl.loop(0, rows // row_tile)
    def _(i):
        start = pl.multiple_of(i * row_tile, row_tile)
        x = normed_ref[pl.ds(start, row_tile), :]
        for n in range(0, channels, 256):
            value = jnp.dot(x, weights[:, n : n + 256], preferred_element_type=jnp.float32)
            gate = jnp.dot(x, weights[:, channels + n : channels + n + 256], preferred_element_type=jnp.float32)
            product = (value * sigmoid(gate)).astype(jnp.bfloat16).astype(jnp.float32)
            for g in range(2):
                gated[n // LANES + g, pl.ds(halo + start, row_tile), :] = product[:, g * LANES : (g + 1) * LANES]

    block = 64
    for g in range(groups):
        lanes = slice(g * LANES, (g + 1) * LANES)

        def body(i, total):
            start = pl.multiple_of(i * block, block)
            summed = jnp.zeros((block, LANES), jnp.float32)
            for o in range(n_taps):
                summed = summed + gated[g, pl.ds(start + (halo - half + o), block), :] * taps_ref[o : o + 1, lanes]
            conv_ref[pl.ds(start, block), lanes] = summed
            kept = summed * mask_ref[pl.ds(start, block), :]
            return total + jnp.sum(kept.reshape(block // 8, 8, LANES), axis=0)

        total = lax.fori_loop(0, rows // block, body, jnp.zeros((8, LANES), jnp.float32))
        average = jnp.sum(total, axis=0, keepdims=True) / count_ref[0]

        def body2(i, total):
            start = pl.multiple_of(i * block, block)
            centred = (conv_ref[pl.ds(start, block), lanes] - average) * mask_ref[pl.ds(start, block), :]
            return total + jnp.sum((centred * centred).reshape(block // 8, 8, LANES), axis=0)

        total = lax.fori_loop(0, rows // block, body2, jnp.zeros((8, LANES), jnp.float32))
        stats_ref[0:1, lanes] = average
        stats_ref[1:2, lanes] = jnp.sum(total, axis=0, keepdims=True)


def out_kernel(*refs, n_conv, n_pieces, utterances, row_tile):
    places_ref, lengths_ref, frames_ref, average_ref, scale_ref, shift_ref = refs[:6]
    convs = refs[6 : 6 + n_conv]
    pieces = refs[6 + n_conv : 6 + n_conv + n_pieces]
    out_ref, weights, active = refs[6 + n_conv + n_pieces :]
    rows, features = frames_ref.shape
    bounds = row_bounds(lengths_ref, utterances)
    reorder(places_ref, pieces, weights)

    @pl.loop(0, rows // row_tile)
    def _(i):
        start = pl.multiple_of(i * row_tile, row_tile)
        for k in range(row_tile // GAP):
            first = pl.multiple_of(start + k * GAP, GAP)
            row = lax.broadcasted_iota(jnp.int32, (GAP, 1), 0) + first
            at = 0
            for conv in convs:
                width = conv.shape[1]
                values = conv[pl.ds(first, GAP), :]
                for u in range(1, utterances):
                    moved = conv[pl.ds(pl.multiple_of(first + u * GAP, GAP), GAP), :]
                    values = jnp.where(row >= bounds[u], moved, values)
                lanes = slice(at, at + width)
                scaled = (values - average_ref[0:1, lanes]) * scale_ref[0:1, lanes] + shift_ref[0:1, lanes]
                active[k * GAP : (k + 1) * GAP, lanes] = (scaled * sigmoid(scaled)).astype(active.dtype)
                at += width
        row = lax.broadcasted_iota(jnp.int32, (row_tile, 1), 0) + start
        live = row < bounds[utterances]
        for n in range(0, features, 512):
            branch = jnp.dot(active[...], weights[:, n : n + 512], preferred_element_type=jnp.float32)
            mixed = frames_ref[pl.ds(start, row_tile), n : n + 512].astype(jnp.float32) + branch
            out_ref[pl.ds(start, row_tile), n : n + 512] = jnp.where(live, mixed, 0.0).astype(out_ref.dtype)


SMEM = pl.BlockSpec(memory_space=pltpu.SMEM)
VMEM = pl.BlockSpec(memory_space=pltpu.VMEM)
PARAMS = pltpu.CompilerParams(vmem_limit_bytes=VMEM_LIMIT)


def normalise(frames, lengths, gain, bias, padded_rows):
    utterances = lengths.shape[0]
    rows, features = frames.shape
    lead = (utterances - 1) * GAP
    return pl.pallas_call(
        functools.partial(norm_kernel, utterances=utterances),
        out_shape=(
            jax.ShapeDtypeStruct((padded_rows, features), jnp.bfloat16),
            jax.ShapeDtypeStruct((padded_rows, LANES), jnp.float32),
        ),
        in_specs=[SMEM, VMEM, VMEM, VMEM],
        out_specs=(VMEM, VMEM),
        scratch_shapes=[pltpu.VMEM((lead + padded_rows, features), jnp.bfloat16)],
        compiler_params=PARAMS,
        name="normalise",
    )(lengths, frames, gain[None], bias[None])


def chunk(places, count, normed, mask, taps, pieces):
    rows, depth = normed.shape
    channels = pieces[0].shape[1] // 2
    halo = 16
    flops = 2 * rows * depth * channels * 2
    return pl.pallas_call(
        functools.partial(chunk_kernel, n_pieces=len(pieces), row_tile=rows // 3, halo=halo),
        out_shape=(
            jax.ShapeDtypeStruct((rows, channels), jnp.float32),
            jax.ShapeDtypeStruct((2, channels), jnp.float32),
        ),
        in_specs=[SMEM, SMEM] + [VMEM] * (3 + len(pieces)),
        out_specs=(VMEM, VMEM),
        scratch_shapes=[
            pltpu.VMEM((depth, 2 * channels), jnp.bfloat16),
            pltpu.VMEM((channels // LANES, rows + 2 * halo, LANES), jnp.float32),
        ],
        compiler_params=PARAMS,
        cost_estimate=pl.CostEstimate(flops=4 * flops, bytes_accessed=4 * rows * channels, transcendentals=0),
        name="chunk",
    )(places, count, normed, mask, taps, *pieces)


def finish(places, lengths, frames, average, scale, shift, convs, pieces):
    rows, features = frames.shape
    row_tile = 128 if rows % 128 == 0 else GAP
    return pl.pallas_call(
        functools.partial(
            out_kernel,
            n_conv=len(convs),
            n_pieces=len(pieces),
            utterances=lengths.shape[0],
            row_tile=row_tile,
        ),
        out_shape=jax.ShapeDtypeStruct((rows, features), jnp.bfloat16),
        in_specs=[SMEM, SMEM] + [VMEM] * (4 + len(convs) + len(pieces)),
        out_specs=VMEM,
        scratch_shapes=[
            pltpu.VMEM((features, features), jnp.bfloat16),
            pltpu.VMEM((row_tile, features), jnp.bfloat16),
        ],
        compiler_params=PARAMS,
        name="finish",
    )(places, lengths, frames, average, scale, shift, *convs, *pieces)


def merged_stats(grid, count, average, deviation):
    held = jnp.concatenate([average, deviation, jnp.broadcast_to(count, average.shape)], axis=0)
    steps = []
    if grid.c == 2:
        steps.append(lambda z, x, y, c: (z, x, y, c ^ 1))
    for size, move in (
        (grid.x, lambda b: lambda z, x, y, c: (z, x ^ b, y, c)),
        (grid.y, lambda b: lambda z, x, y, c: (z, x, y ^ b, c)),
        (grid.z, lambda b: lambda z, x, y, c: (z ^ b, x, y, c)),
    ):
        bit = 1
        while bit < size:
            steps.append(move(bit))
            bit *= 2
    for step in steps:
        other = lax.ppermute(held, AXES, grid.pairs(step))
        total = held[2:3] + other[2:3]
        delta = other[0:1] - held[0:1]
        share = other[2:3] / total
        held = jnp.concatenate(
            [
                held[0:1] + delta * share,
                held[1:2] + other[1:2] + delta * delta * held[2:3] * share,
                total,
            ],
            axis=0,
        )
    return held[0:1], held[1:2]


def on_device(grid, frames_in, lengths, norm_gain, norm_bias, w_in, kernel, batch_gain, batch_bias, w_out):
    frames = frames_in[0]
    lengths = lengths[0, 0]
    capacity, features = frames.shape
    utterances = lengths.shape[0]
    total_count = grid.count * FR_DEV
    me = lax.axis_index(AXES)
    padded_rows = round_up(capacity + GAP * (utterances - 1), 192)
    part = features // 3
    parts = range(0, features, part)
    shards = [jnp.concatenate([w_in[:, at : at + part], w_in[:, features + at : features + at + part]], axis=1) for at in parts]
    if w_in.shape[0] % 16 == 0:
        held = [gather(grid, shard, True) for shard in shards]
        held_out = gather(grid, w_out, False)
        in_places = place_of(held[0], me)
        out_places = place_of(held_out, me)
        gathered = [[h.value for h in pieces] for pieces in held]
        gathered_out = [h.value for h in held_out]
    else:
        gathered = [[lax.all_gather(shard, AXES, axis=0, tiled=True)] for shard in shards]
        gathered_out = [lax.all_gather(w_out, AXES, axis=0, tiled=True)]
        in_places = out_places = jnp.zeros((1,), jnp.int32)
    normed, mask = normalise(frames, lengths, norm_gain, norm_bias, padded_rows)
    count = jnp.sum(lengths).astype(jnp.float32)
    convs, stats = [], []
    for at, pieces in zip(parts, gathered):
        conv, stat = chunk(in_places, count[None], normed, mask, kernel[:, at : at + part], pieces)
        convs.append(conv)
        stats.append(stat)
    stats = jnp.concatenate(stats, axis=1)
    average, deviation = merged_stats(grid, count, stats[0:1], stats[1:2])
    spread = deviation / total_count
    scale = lax.rsqrt(spread + EPSILON) * batch_gain[None]
    result = finish(out_places, lengths, frames, average, scale, batch_bias[None], convs, gathered_out)
    return result[None]


def solution(mesh):
    grid = Grid(mesh.shape["dp"], mesh.shape["rep"])
    placed = (
        P("rep", "dp", None),
        P("rep", "dp", None),
        P(),
        P(),
        P(("dp", "rep"), None),
        P(),
        P(),
        P(),
        P(("dp", "rep"), None),
    )
    return jax.shard_map(
        functools.partial(on_device, grid),
        mesh=mesh,
        in_specs=placed,
        out_specs=P("rep", "dp", None),
        check_vma=False,
    )
```

time: 247 us -> 179 us (0.72)
  blocking collectives: 79.5 us -> 0 us
  Pallas kernels: 0 us -> 57 us
  other arithmetic: 49.9 us -> 7.8 us
  matrix products: 21.9 us -> 0 us
  starting transfers between devices: 0.04 us -> 18.6 us
  local copies, waits for them, and re-layouts: 3.21 us -> 17.6 us
  between operations: 13.5 us -> 1.22 us
  waiting for transfers between devices: 78.4 us -> 75.8 us
    psum x2 -> x0, blocking collectives: 79.5 us -> none  [the longest x1 40.2 us: on_device(): lax.psum(jnp.sum(centred * centred * row_weight, axis=0), ('dp', 'rep'))]
    all_gather x2 -> x0, waiting for transfers between devices: 77 us -> none  [the longest x1 77 us: on_device(): lax.all_gather(w_in, ('dp', 'rep'), axis=0, tiled=True)]
    ppermute x0 -> x29, waiting for transfers between devices: none -> 75.8 us  [the longest x24 65 us: sent(): return Held(lax.ppermute(self.value, AXES, pairs), owners)]
    pallas_call x0 -> x5, Pallas kernels: none -> 57 us  [the longest x3 36.4 us: chunk(): pl.pallas_call(functools.partial(chunk_kernel, n_pieces=len(pieces), row_...]
    reduce_sum x6 -> x1, other arithmetic: 45.9 us -> 0.66 us  [on_device(): count = jnp.sum(lengths).astype(jnp.float32)]
    dot_general x2 -> x0, matrix products: 21.9 us -> none  [the longest x1 11.4 us: project_in(): return jnp.dot(normed, weight_rows, preferred_element_type=jnp.float32)]
    ppermute x0 -> x29, starting transfers between devices: none -> 18.6 us  [the longest x24 16.4 us: sent(): return Held(lax.ppermute(self.value, AXES, pairs), owners)]
    unnamed x12 -> x60, local copies, waits for them, and re-layouts: 0.03 us -> 13 us
  transfers between devices with their start and end apart: 2 -> 29, of which waited for: 1 -> 14; matrix products, arithmetic and copies ran while one was open for 26% -> 12% of each run, Pallas kernels for 0% -> 25%
where the time goes in v1:
time: 179 us; the launch traced here: 178 us
  waiting for transfers between devices  75.8 us (42%)
  Pallas kernels  57 us (32%)
  starting transfers between devices  18.6 us (10%)
  local copies, waits for them, and re-layouts  17.6 us (10%)
  other arithmetic  7.8 us (4%)
    ppermute x24, waiting for transfers between devices, sent(): return Held(lax.ppermute(self.value, AXES, pairs), owners)  65 us
    pallas_call x3, Pallas kernels, chunk(): pl.pallas_call(functools.partial(chunk_kernel, n_pieces=len(pieces), row_...  36.4 us
    ppermute x24, starting transfers between devices, sent(): return Held(lax.ppermute(self.value, AXES, pairs), owners)  16.4 us
    unnamed x60, local copies, waits for them, and re-layouts  13 us
    pallas_call x1, Pallas kernels, finish(): pl.pallas_call(functools.partial(out_kernel, n_conv=len(convs), n_pieces=...  11.8 us
    ppermute x5, waiting for transfers between devices, merged_stats(): other = lax.ppermute(held, AXES, grid.pairs(step))  10.7 us
    pallas_call x1, Pallas kernels, normalise(): pl.pallas_call(functools.partial(norm_kernel, utterances=utterances), out...  8.8 us
    concatenate x5, other arithmetic, joined(): return Held(jnp.concatenate([p.value for p in parts], axis=0), owners)  4.66 us
  transfers between devices with their start and end apart: 29, of which 14 were waited for; matrix products, arithmetic and copies ran while one was open for 12% of the time, Pallas kernels for 25%

profile of v1, /device:TPU:0, one launch (start us, length us, event | category | flops | bytes accessed | tf_op | source)
XLA Modules:
  0.0 178.0 jit_solution(4933399780378553691)
XLA Ops:
  1.9 3.0 %collective-permute-start.12 = (bf16[48,1024]{1,0:T(8,128)(2,1)S(1)}, bf16[48,1024]{1,0:T(8,128)(2,1)S(1)}, u32[]{:S(2)}, u32[]{:S(2)}) collective-permute-start(bf16[48,1024]{1,0:T(8,128)(2,1)S(1)} %get-tuple-element.58), channel_id=1, source_target_pairs={{0,8},{1,9},{2,10},{3,11},{4,12},{5,13},{6,14},{7,15},{8,16},{9,17... | collective-permute-start | bytes 294920 | tf_op jit(solution)/shard_map/ppermute | solution.py:51
  5.6 1.6 collective-permute-start.6
  7.2 2.7 %collective-permute-done.12 = bf16[48,1024]{1,0:T(8,128)(2,1)S(1)} collective-permute-done((bf16[48,1024]{1,0:T(8,128)(2,1)S(1)}, bf16[48,1024]{1,0:T(8,128)(2,1)S(1)}, u32[]{:S(2)}, u32[]{:S(2)}) %collective-permute-start.12) | collective-permute-done | bytes 98336 | tf_op jit(solution)/shard_map/ppermute | solution.py:51
  13.5 3.1 %collective-permute-done.13 = bf16[48,1024]{1,0:T(8,128)(2,1)S(1)} collective-permute-done((bf16[48,1024]{1,0:T(8,128)(2,1)S(1)}, bf16[48,1024]{1,0:T(8,128)(2,1)S(1)}, u32[]{:S(2)}, u32[]{:S(2)}) %collective-permute-start.13) | collective-permute-done | bytes 98336 | tf_op jit(solution)/shard_map/ppermute | solution.py:51
  16.7 6.4 %collective-permute-done.14 = bf16[48,1024]{1,0:T(8,128)(2,1)S(1)} collective-permute-done((bf16[48,1024]{1,0:T(8,128)(2,1)S(1)}, bf16[48,1024]{1,0:T(8,128)(2,1)S(1)}, u32[]{:S(2)}, u32[]{:S(2)}) %collective-permute-start.14) | collective-permute-done | bytes 98336 | tf_op jit(solution)/shard_map/ppermute | solution.py:51
  25.1 1.6 constant_dynamic-update-slice_fusion.41
  28.1 8.8 %normalise.1 = (bf16[960,1536]{1,0:T(8,128)(2,1)S(1)}, f32[960,128]{1,0:T(8,128)S(1)}) custom-call(s32[4]{0:T(128)S(1)} %bitcast.10, bf16[896,1536]{1,0:T(8,128)(2,1)S(1)} %bitcast.9, f32[1,1536]{1,0:T(1,128)S(1)} %broadcast_in_dim.24.gain_ref, f32[1,1536]{1,0:T(1,128)S(1)} %broadcast_in_dim.25.bias_ref), custom_call_target="tpu_custom_call" | custom-call | tf_op jit(solution)/shard_map/normalise/pallas_call | solution.py:242
  38.9 1.9 %constant_dynamic-update-slice_fusion.22 = (bf16[384,1024]{1,0:T(8,128)(2,1)}, bf16[768,1024]{1,0:T(8,128)(2,1)S(1)}) fusion(bf16[384,1024]{1,0:T(8,128)(2,1)} %get-tuple-element.50, bf16[192,1024]{1,0:T(8,128)(2,1)} %collective-permute-done.15, bf16[768,1024]{1,0:T(8,128)(2,1)S(1)} %get-tuple-element.51), kind=kLoop, calls=%fused_computation.30 | loop fusion | bytes 1179648 | tf_op jit(solution)/shard_map/concatenate | solution.py:56
  44.6 6.0 %collective-permute-done.7 = bf16[48,1024]{1,0:T(8,128)(2,1)S(1)} collective-permute-done((bf16[48,1024]{1,0:T(8,128)(2,1)}, bf16[48,1024]{1,0:T(8,128)(2,1)S(1)}, u32[]{:S(2)}, u32[]{:S(2)}) %collective-permute-start.7) | collective-permute-done | bytes 98336 | tf_op jit(solution)/shard_map/ppermute | solution.py:51
  52.8 4.3 %collective-permute-done.8 = bf16[48,1024]{1,0:T(8,128)(2,1)S(1)} collective-permute-done((bf16[48,1024]{1,0:T(8,128)(2,1)S(1)}, bf16[48,1024]{1,0:T(8,128)(2,1)S(1)}, u32[]{:S(2)}, u32[]{:S(2)}) %collective-permute-start.8) | collective-permute-done | bytes 98336 | tf_op jit(solution)/shard_map/ppermute | solution.py:51
  62.6 3.3 %collective-permute-done.9 = bf16[192,1024]{1,0:T(8,128)(2,1)S(1)} collective-permute-done((bf16[192,1024]{1,0:T(8,128)(2,1)S(1)}, bf16[192,1024]{1,0:T(8,128)(2,1)S(1)}, u32[]{:S(2)}, u32[]{:S(2)}) %collective-permute-start.9) | collective-permute-done | bytes 393248 | tf_op jit(solution)/shard_map/ppermute | solution.py:51
  67.5 1.6 collective-permute-start.24
  69.1 5.1 %collective-permute-done.3 = bf16[192,1024]{1,0:T(8,128)(2,1)S(1)} collective-permute-done((bf16[192,1024]{1,0:T(8,128)(2,1)S(1)}, bf16[192,1024]{1,0:T(8,128)(2,1)S(1)}, u32[]{:S(2)}, u32[]{:S(2)}) %collective-permute-start.3) | collective-permute-done | bytes 393248 | tf_op jit(solution)/shard_map/ppermute | solution.py:51
  74.9 6.2 %collective-permute-done.24 = bf16[96,1536]{1,0:T(8,128)(2,1)S(1)} collective-permute-done((bf16[96,1536]{1,0:T(8,128)(2,1)S(1)}, bf16[96,1536]{1,0:T(8,128)(2,1)S(1)}, u32[]{:S(2)}, u32[]{:S(2)}) %collective-permute-start.24) | collective-permute-done | bytes 294944 | tf_op jit(solution)/shard_map/ppermute | solution.py:51
  83.0 1.6 constant_dynamic-update-slice_fusion.40
  85.3 14.7 %collective-permute-done.25 = bf16[192,1536]{1,0:T(8,128)(2,1)} collective-permute-done((bf16[192,1536]{1,0:T(8,128)(2,1)S(1)}, bf16[192,1536]{1,0:T(8,128)(2,1)}, u32[]{:S(2)}, u32[]{:S(2)}) %collective-permute-start.25) | collective-permute-done | bytes 589856 | tf_op jit(solution)/shard_map/ppermute | solution.py:51
  100.1 12.1 %chunk.5 = (f32[960,512]{1,0:T(8,128)S(1)}, f32[2,512]{1,0:T(2,128)S(1)}) custom-call(s32[32]{0:T(128)S(1)} %dynamic-slice_bitcast_fusion.refs_0_, f32[1]{0:T(128)} %bitcast.4.refs_1_, bf16[960,1536]{1,0:T(8,128)(2,1)} %copy-done.5, f32[960,128]{1,0:T(8,128)S(1)} %get-tuple-element.14.refs_3_, f32[31,512]{1,0:T(8,128)S(1)} %get-tuple-element.47.refs_4_, ...), custom_call_target="tpu_custom_call" | custom-call | flops 12079595520 | bytes 1966080 | tf_op jit(solution)/shard_map/chunk/pallas_call | solution.py:261
  112.2 12.1 %chunk.4 = (f32[960,512]{1,0:T(8,128)S(1)}, f32[2,512]{1,0:T(2,128)S(1)}) custom-call(s32[32]{0:T(128)S(1)} %dynamic-slice_bitcast_fusion.refs_0_, f32[1]{0:T(128)} %bitcast.4.refs_1_, bf16[960,1536]{1,0:T(8,128)(2,1)} %copy-done.5, f32[960,128]{1,0:T(8,128)S(1)} %get-tuple-element.14.refs_3_, f32[31,512]{1,0:T(8,128)S(1)} %get-tuple-element.49.refs_4_, ...), custom_call_target="tpu_custom_call" | custom-call | flops 12079595520 | bytes 1966080 | tf_op jit(solution)/shard_map/chunk/pallas_call | solution.py:261
  124.3 12.2 %chunk.3 = (f32[960,512]{1,0:T(8,128)S(1)}, f32[2,512]{1,0:T(2,128)S(1)}) custom-call(s32[32]{0:T(128)S(1)} %dynamic-slice_bitcast_fusion.refs_0_, f32[1]{0:T(128)} %bitcast.4.refs_1_, bf16[960,1536]{1,0:T(8,128)(2,1)} %copy-done.5, f32[960,128]{1,0:T(8,128)S(1)} %get-tuple-element.14.refs_3_, f32[31,512]{1,0:T(8,128)S(1)} %get-tuple-element.48.refs_4_, ...), custom_call_target="tpu_custom_call" | custom-call | flops 12079595520 | bytes 1966080 | tf_op jit(solution)/shard_map/chunk/pallas_call | solution.py:261
  139.1 3.2 %collective-permute-done.19 = f32[3,1536]{1,0:T(4,128)S(1)} collective-permute-done((f32[3,1536]{1,0:T(4,128)S(1)}, f32[3,1536]{1,0:T(4,128)S(1)}, u32[]{:S(2)}, u32[]{:S(2)}) %collective-permute-start.19) | collective-permute-done | bytes 18464 | tf_op jit(solution)/shard_map/ppermute | solution.py:317
  143.0 12.7 %collective-permute-done.27 = bf16[192,1536]{1,0:T(8,128)(2,1)S(1)} collective-permute-done((bf16[192,1536]{1,0:T(8,128)(2,1)S(1)}, bf16[192,1536]{1,0:T(8,128)(2,1)S(1)}, u32[]{:S(2)}, u32[]{:S(2)}) %collective-permute-start.27) | collective-permute-done | bytes 589856 | tf_op jit(solution)/shard_map/ppermute | solution.py:51
  156.0 3.8 %collective-permute-done.21 = f32[3,1536]{1,0:T(4,128)S(1)} collective-permute-done((f32[3,1536]{1,0:T(4,128)S(1)}, f32[3,1536]{1,0:T(4,128)S(1)}, u32[]{:S(2)}, u32[]{:S(2)}) %collective-permute-start.21) | collective-permute-done | bytes 18464 | tf_op jit(solution)/shard_map/ppermute | solution.py:317
  161.0 3.7 %collective-permute-done.22 = f32[3,1536]{1,0:T(4,128)S(1)} collective-permute-done((f32[3,1536]{1,0:T(4,128)S(1)}, f32[3,1536]{1,0:T(4,128)S(1)}, u32[]{:S(2)}, u32[]{:S(2)}) %collective-permute-start.22) | collective-permute-done | bytes 18464 | tf_op jit(solution)/shard_map/ppermute | solution.py:317
  166.2 11.8 %finish.1 = bf16[896,1536]{1,0:T(8,128)(2,1)} custom-call(s32[32]{0:T(128)S(1)} %dynamic-slice_bitcast_fusion.1.refs_0_, s32[4]{0:T(128)S(1)} %bitcast.11, bf16[896,1536]{1,0:T(8,128)(2,1)} %bitcast.8, f32[1,1536]{1,0:T(1,128)S(1)} %multiply_add_fusion.refs_3_, f32[1,1536]{1,0:T(1,128)S(1)} %get-tuple-element.21.refs_4_, ...), custom_call_target="tpu_custom_call" | custom-call | tf_op jit(solution)/shard_map/finish/pallas_call | solution.py:282
  (138 shorter events, 33.4 us)
Async XLA Ops:
  1.9 8.0 %collective-permute-start.12 = (bf16[48,1024]{1,0:T(8,128)(2,1)S(1)}, bf16[48,1024]{1,0:T(8,128)(2,1)S(1)}, u32[]{:S(2)}, u32[]{:S(2)}) collective-permute-start(bf16[48,1024]{1,0:T(8,128)(2,1)S(1)} %get-tuple-element.58), channel_id=1, source_target_pairs={{0,8},{1,9},{2,10},{3,11},{4,12},{5,13},{6,14},{7,15},{8,16},{9,17... | collective-permute-start | bytes 294920 | tf_op jit(solution)/shard_map/ppermute | solution.py:51
  5.6 37.4 %collective-permute-start.6 = (bf16[48,1024]{1,0:T(8,128)(2,1)S(1)}, bf16[48,1024]{1,0:T(8,128)(2,1)}, u32[]{:S(2)}, u32[]{:S(2)}) collective-permute-start(bf16[48,1024]{1,0:T(8,128)(2,1)S(1)} %get-tuple-element.67), channel_id=1, source_target_pairs={{0,8},{1,9},{2,10},{3,11},{4,12},{5,13},{6,14},{7,15},{8,16},{9,17... | collective-permute-start | bytes 294920 | tf_op jit(solution)/shard_map/ppermute | solution.py:51
  9.9 6.7 %collective-permute-start.13 = (bf16[48,1024]{1,0:T(8,128)(2,1)S(1)}, bf16[48,1024]{1,0:T(8,128)(2,1)S(1)}, u32[]{:S(2)}, u32[]{:S(2)}) collective-permute-start(bf16[48,1024]{1,0:T(8,128)(2,1)S(1)} %collective-permute-done.12), channel_id=1, source_target_pairs={{0,8},{1,9},{2,10},{3,11},{4,12},{5,13},{6,14},{7,15},{8,16},{9,17... | collective-permute-start | bytes 294920 | tf_op jit(solution)/shard_map/ppermute | solution.py:51
  10.6 32.4 %collective-permute-start = (bf16[48,1024]{1,0:T(8,128)(2,1)S(1)}, bf16[48,1024]{1,0:T(8,128)(2,1)}, u32[]{:S(2)}, u32[]{:S(2)}) collective-permute-start(bf16[48,1024]{1,0:T(8,128)(2,1)S(1)} %get-tuple-element.76), channel_id=1, source_target_pairs={{0,8},{1,9},{2,10},{3,11},{4,12},{5,13},{6,14},{7,15},{8,16},{9,17... | collective-permute-start | bytes 294920 | tf_op jit(solution)/shard_map/ppermute | solution.py:51
  12.0 54.5 %collective-permute-start.23 = (bf16[48,1536]{1,0:T(8,128)(2,1)}, bf16[48,1536]{1,0:T(8,128)(2,1)}, u32[]{:S(2)}, u32[]{:S(2)}) collective-permute-start(bf16[48,1536]{1,0:T(8,128)(2,1)} %param.19), channel_id=1, source_target_pairs={{0,4},{1,3},{2,6},{3,1},{4,0},{5,7},{6,2},{7,5},{8,12},{9,11},{10,... | collective-permute-start | bytes 442376 | tf_op jit(solution)/shard_map/ppermute | solution.py:51
  16.6 6.5 %collective-permute-start.14 = (bf16[48,1024]{1,0:T(8,128)(2,1)S(1)}, bf16[48,1024]{1,0:T(8,128)(2,1)S(1)}, u32[]{:S(2)}, u32[]{:S(2)}) collective-permute-start(bf16[48,1024]{1,0:T(8,128)(2,1)S(1)} %collective-permute-done.13), channel_id=1, source_target_pairs={{0,8},{1,9},{2,10},{3,11},{4,12},{5,13},{6,14},{7,15},{8,16},{9,17... | collective-permute-start | bytes 294920 | tf_op jit(solution)/shard_map/ppermute | solution.py:51
  23.8 15.1 %collective-permute-start.15 = (bf16[192,1024]{1,0:T(8,128)(2,1)}, bf16[192,1024]{1,0:T(8,128)(2,1)}, u32[]{:S(2)}, u32[]{:S(2)}) collective-permute-start(bf16[192,1024]{1,0:T(8,128)(2,1)} %pad_maximum_fusion.3), channel_id=1, source_target_pairs={{0,4},{1,3},{2,6},{3,1},{4,0},{5,7},{6,2},{7,5},{8,12},{9,11},{10,... | collective-permute-start | bytes 1179656 | tf_op jit(solution)/shard_map/ppermute | solution.py:51
  40.8 21.7 %collective-permute-start.16 = (bf16[384,1024]{1,0:T(8,128)(2,1)}, bf16[384,1024]{1,0:T(8,128)(2,1)S(1)}, u32[]{:S(2)}, u32[]{:S(2)}) collective-permute-start(bf16[384,1024]{1,0:T(8,128)(2,1)} %get-tuple-element.35), channel_id=1, source_target_pairs={{0,2},{1,5},{2,0},{3,7},{4,6},{5,1},{6,4},{7,3},{8,10},{9,13},{10,... | collective-permute-start | bytes 2359304 | tf_op jit(solution)/shard_map/ppermute | solution.py:51
  43.0 7.7 %collective-permute-start.7 = (bf16[48,1024]{1,0:T(8,128)(2,1)}, bf16[48,1024]{1,0:T(8,128)(2,1)S(1)}, u32[]{:S(2)}, u32[]{:S(2)}) collective-permute-start(bf16[48,1024]{1,0:T(8,128)(2,1)} %collective-permute-done.6), channel_id=1, source_target_pairs={{0,8},{1,9},{2,10},{3,11},{4,12},{5,13},{6,14},{7,15},{8,16},{9,17... | collective-permute-start | bytes 294920 | tf_op jit(solution)/shard_map/ppermute | solution.py:51
  43.0 9.8 %collective-permute-start.1 = (bf16[48,1024]{1,0:T(8,128)(2,1)}, bf16[48,1024]{1,0:T(8,128)(2,1)S(1)}, u32[]{:S(2)}, u32[]{:S(2)}) collective-permute-start(bf16[48,1024]{1,0:T(8,128)(2,1)} %collective-permute-done), channel_id=1, source_target_pairs={{0,8},{1,9},{2,10},{3,11},{4,12},{5,13},{6,14},{7,15},{8,16},{9,17... | collective-permute-start | bytes 294920 | tf_op jit(solution)/shard_map/ppermute | solution.py:51
  52.7 6.5 %collective-permute-start.2 = (bf16[48,1024]{1,0:T(8,128)(2,1)S(1)}, bf16[48,1024]{1,0:T(8,128)(2,1)S(1)}, u32[]{:S(2)}, u32[]{:S(2)}) collective-permute-start(bf16[48,1024]{1,0:T(8,128)(2,1)S(1)} %collective-permute-done.1), channel_id=1, source_target_pairs={{0,8},{1,9},{2,10},{3,11},{4,12},{5,13},{6,14},{7,15},{8,16},{9,17... | collective-permute-start | bytes 294920 | tf_op jit(solution)/shard_map/ppermute | solution.py:51
  58.0 7.8 %collective-permute-start.9 = (bf16[192,1024]{1,0:T(8,128)(2,1)S(1)}, bf16[192,1024]{1,0:T(8,128)(2,1)S(1)}, u32[]{:S(2)}, u32[]{:S(2)}) collective-permute-start(bf16[192,1024]{1,0:T(8,128)(2,1)S(1)} %pad_maximum_fusion.2), channel_id=1, source_target_pairs={{0,4},{1,3},{2,6},{3,1},{4,0},{5,7},{6,2},{7,5},{8,12},{9,11},{10,... | collective-permute-start | bytes 1179656 | tf_op jit(solution)/shard_map/ppermute | solution.py:51
  60.2 14.1 %collective-permute-start.3 = (bf16[192,1024]{1,0:T(8,128)(2,1)S(1)}, bf16[192,1024]{1,0:T(8,128)(2,1)S(1)}, u32[]{:S(2)}, u32[]{:S(2)}) collective-permute-start(bf16[192,1024]{1,0:T(8,128)(2,1)S(1)} %pad_maximum_fusion.1), channel_id=1, source_target_pairs={{0,4},{1,3},{2,6},{3,1},{4,0},{5,7},{6,2},{7,5},{8,12},{9,11},{10,... | collective-permute-start | bytes 1179656 | tf_op jit(solution)/shard_map/ppermute | solution.py:51
  62.5 37.6 %collective-permute-start.17 = (bf16[768,1024]{1,0:T(8,128)(2,1)S(1)}, bf16[768,1024]{1,0:T(8,128)(2,1)S(1)}, u32[]{:S(2)}, u32[]{:S(2)}) collective-permute-start(bf16[768,1024]{1,0:T(8,128)(2,1)S(1)} %constant_dynamic-update-slice_fusion.27.refs_5_), channel_id=1, source_target_pairs={{0,1},{1,0},{2,3},{3,2},{4,5},{5,4},{6,7},{7,6},{8,9},{9,8},{10,11... | collective-permute-start | bytes 4718600 | tf_op jit(solution)/shard_map/ppermute | solution.py:51
  65.9 16.3 %collective-permute-start.10 = (bf16[384,1024]{1,0:T(8,128)(2,1)S(1)}, bf16[384,1024]{1,0:T(8,128)(2,1)S(1)}, u32[]{:S(2)}, u32[]{:S(2)}) collective-permute-start(bf16[384,1024]{1,0:T(8,128)(2,1)S(1)} %get-tuple-element.37), channel_id=1, source_target_pairs={{0,2},{1,5},{2,0},{3,7},{4,6},{5,1},{6,4},{7,3},{8,10},{9,13},{10,... | collective-permute-start | bytes 2359304 | tf_op jit(solution)/shard_map/ppermute | solution.py:51
  67.5 13.6 %collective-permute-start.24 = (bf16[96,1536]{1,0:T(8,128)(2,1)S(1)}, bf16[96,1536]{1,0:T(8,128)(2,1)S(1)}, u32[]{:S(2)}, u32[]{:S(2)}) collective-permute-start(bf16[96,1536]{1,0:T(8,128)(2,1)S(1)} %pad_maximum_fusion.4), channel_id=1, source_target_pairs={{0,2},{1,5},{2,0},{3,7},{4,6},{5,1},{6,4},{7,3},{8,10},{9,13},{10,... | collective-permute-start | bytes 884744 | tf_op jit(solution)/shard_map/ppermute | solution.py:51
  74.3 25.7 %collective-permute-start.4 = (bf16[384,1024]{1,0:T(8,128)(2,1)S(1)}, bf16[384,1024]{1,0:T(8,128)(2,1)S(1)}, u32[]{:S(2)}, u32[]{:S(2)}) collective-permute-start(bf16[384,1024]{1,0:T(8,128)(2,1)S(1)} %get-tuple-element.39), channel_id=1, source_target_pairs={{0,2},{1,5},{2,0},{3,7},{4,6},{5,1},{6,4},{7,3},{8,10},{9,13},{10,... | collective-permute-start | bytes 2359304 | tf_op jit(solution)/shard_map/ppermute | solution.py:51
  82.2 17.8 %collective-permute-start.25 = (bf16[192,1536]{1,0:T(8,128)(2,1)S(1)}, bf16[192,1536]{1,0:T(8,128)(2,1)}, u32[]{:S(2)}, u32[]{:S(2)}) collective-permute-start(bf16[192,1536]{1,0:T(8,128)(2,1)S(1)} %pad_maximum_fusion), channel_id=1, source_target_pairs={{0,8},{1,9},{2,10},{3,11},{4,12},{5,13},{6,14},{7,15},{8,16},{9,17... | collective-permute-start | bytes 1769480 | tf_op jit(solution)/shard_map/ppermute | solution.py:51
  82.3 29.9 %collective-permute-start.11 = (bf16[768,1024]{1,0:T(8,128)(2,1)S(1)}, bf16[768,1024]{1,0:T(8,128)(2,1)S(1)}, u32[]{:S(2)}, u32[]{:S(2)}) collective-permute-start(bf16[768,1024]{1,0:T(8,128)(2,1)S(1)} %constant_dynamic-update-slice_fusion.16.refs_5_), channel_id=1, source_target_pairs={{0,1},{1,0},{2,3},{3,2},{4,5},{5,4},{6,7},{7,6},{8,9},{9,8},{10,11... | collective-permute-start | bytes 4718600 | tf_op jit(solution)/shard_map/ppermute | solution.py:51
  100.0 38.3 %collective-permute-start.26 = (bf16[192,1536]{1,0:T(8,128)(2,1)}, bf16[192,1536]{1,0:T(8,128)(2,1)S(1)}, u32[]{:S(2)}, u32[]{:S(2)}) collective-permute-start(bf16[192,1536]{1,0:T(8,128)(2,1)} %collective-permute-done.25), channel_id=1, source_target_pairs={{0,8},{1,9},{2,10},{3,11},{4,12},{5,13},{6,14},{7,15},{8,16},{9,17... | collective-permute-start | bytes 1769480 | tf_op jit(solution)/shard_map/ppermute | solution.py:51
  100.1 24.3 %collective-permute-start.5 = (bf16[768,1024]{1,0:T(8,128)(2,1)S(1)}, bf16[768,1024]{1,0:T(8,128)(2,1)S(1)}, u32[]{:S(2)}, u32[]{:S(2)}) collective-permute-start(bf16[768,1024]{1,0:T(8,128)(2,1)S(1)} %constant_dynamic-update-slice_fusion.5.refs_5_), channel_id=1, source_target_pairs={{0,1},{1,0},{2,3},{3,2},{4,5},{5,4},{6,7},{7,6},{8,9},{9,8},{10,11... | collective-permute-start | bytes 4718600 | tf_op jit(solution)/shard_map/ppermute | solution.py:51
  138.3 17.4 %collective-permute-start.27 = (bf16[192,1536]{1,0:T(8,128)(2,1)S(1)}, bf16[192,1536]{1,0:T(8,128)(2,1)S(1)}, u32[]{:S(2)}, u32[]{:S(2)}) collective-permute-start(bf16[192,1536]{1,0:T(8,128)(2,1)S(1)} %collective-permute-done.26), channel_id=1, source_target_pairs={{0,8},{1,9},{2,10},{3,11},{4,12},{5,13},{6,14},{7,15},{8,16},{9,17... | collective-permute-start | bytes 1769480 | tf_op jit(solution)/shard_map/ppermute | solution.py:51
  142.5 13.4 %collective-permute-start.20 = (f32[3,1536]{1,0:T(4,128)S(1)}, f32[3,1536]{1,0:T(4,128)S(1)}, u32[]{:S(2)}, u32[]{:S(2)}) collective-permute-start(f32[3,1536]{1,0:T(4,128)S(1)} %pad_maximum_fusion.9), channel_id=1, source_target_pairs={{0,2},{1,3},{2,0},{3,1},{4,6},{5,7},{6,4},{7,5},{8,10},{9,11},{10,... | collective-permute-start | bytes 55304 | tf_op jit(solution)/shard_map/ppermute | solution.py:317
  155.8 9.0 %collective-permute-start.28 = (bf16[768,1536]{1,0:T(8,128)(2,1)S(1)}, bf16[768,1536]{1,0:T(8,128)(2,1)S(1)}, u32[]{:S(2)}, u32[]{:S(2)}) collective-permute-start(bf16[768,1536]{1,0:T(8,128)(2,1)S(1)} %constant_dynamic-update-slice_fusion.36.refs_9_), channel_id=1, source_target_pairs={{0,1},{1,0},{2,3},{3,2},{4,5},{5,4},{6,7},{7,6},{8,9},{9,8},{10,11... | collective-permute-start | bytes 7077896 | tf_op jit(solution)/shard_map/ppermute | solution.py:51
  (27 other events, 394.6 us)
